TPU v7x, 512 devices: a whole 4x4x16 slice. The times are simulated.
512 devices in a mesh: blk: 64 (over y, z_lo, core), tgt: 8 (over x, z_hi).
Axes of the slice: x: 4, y: 4, z: 16 (z_hi: 2, z_lo: 8; z = z_hi * 8 + z_lo), core: 2. Of those that a mesh axis runs over, the one named last changes fastest.
Arguments:
- history: float32 [32768, 1536], P(('blk', 'tgt')), may hold values from 0 to 2
- weights: bfloat16 [64, 512, 32768], P(None, 'tgt', 'blk'), may hold values from -0.03125 to 0.03125
- delays: int32 [32, 32], replicated, may hold values from 16 to 64
- area_blocks: int32 [32], replicated, may hold values from 1 to 3, 64 in all
- potential: float32 [24, 32768], P(None, ('blk', 'tgt')), may hold values from -6 to 6
- leak: float32 [32768], P(('blk', 'tgt')), may hold values from 0.03 to 0.6
- drive: float32 [32768], P(('blk', 'tgt')), may hold values from -6 to 6
Outputs:
- rate_steps: float32 [16, 24, 32768], P(None, None, ('blk', 'tgt'))
- last_potential: float32 [24, 32768], P(None, ('blk', 'tgt'))
Inputs may be any that keep to these rules, and one draw needn't show every extreme that they name: Area a consists of area_blocks[a] consecutive blocks of 512 neurons; areas follow one another in order.
All inputs are finite; a program needn't handle non-finite values.
Results may differ from a plain program's by a relative error of at most 0.00083.
Values may be sent and summed in bfloat16 or wider, within the bound.
A program may use at most 128 MiB of HBM per device.

v0:
```python
import jax
import jax.numpy as jnp
from jax import lax
from jax.sharding import PartitionSpec as P

STEPS = 16


def cut_along(x, dim, peers):
    lengths = x.shape
    parts = x.reshape(*lengths[:dim], peers, lengths[dim] // peers, *lengths[dim + 1 :])
    return jnp.moveaxis(parts, dim, 0)


def summed_on_arrival(x, axis, dim):
    parts = cut_along(x, dim, lax.axis_size(axis))
    arrived = lax.all_to_all(parts, axis, split_axis=0, concat_axis=0, tiled=True)
    return arrived.sum(axis=0)


def block_areas(area_blocks, block_count):
    boundary = jnp.cumsum(area_blocks)
    blocks = jnp.arange(block_count, dtype=jnp.int32)
    return jnp.sum((boundary[None, :] <= blocks[:, None]).astype(jnp.int32), axis=1)


def on_device(history, weights, delays, area_blocks, potential, leak, drive):
    block_count = weights.shape[0]
    piece_width = weights.shape[1]
    columns = history.shape[1]
    trial_count = potential.shape[0]
    window_width = STEPS * trial_count
    area_of_block = block_areas(area_blocks, block_count)
    my_block = lax.axis_index("blk")
    my_area = area_of_block[my_block]
    history_low = history.astype(jnp.bfloat16)

    def window(lag_step, column):
        start = columns - lag_step * trial_count
        return lax.dynamic_slice_in_dim(column, start, window_width, 1)

    lag_steps = delays[my_area][area_of_block]
    arrived = lax.all_gather(history_low, "blk", axis=0, tiled=True)
    shard_count = arrived.shape[0] // piece_width
    shaped = arrived.reshape(shard_count, piece_width, columns)
    delayed_input = jax.vmap(window, in_axes=(0, 0))(lag_steps, shaped)
    partial_input = jnp.einsum(
        "gyw,gyt->wt", delayed_input, weights, preferred_element_type=jnp.float32
    )
    own_input = summed_on_arrival(partial_input, "tgt", 1)
    own_input = own_input.reshape(STEPS, trial_count, piece_width)

    def advance(membrane_state, synaptic):
        membrane_state = membrane_state + leak * (drive - membrane_state + synaptic)
        return (membrane_state, jax.nn.softplus(membrane_state))

    last_potential, rate_steps = lax.scan(advance, potential, own_input)
    return (rate_steps, last_potential)


def solution(mesh):
    in_specs = (
        P(("blk", "tgt"), None),
        P(None, "tgt", "blk"),
        P(),
        P(),
        P(None, ("blk", "tgt")),
        P(("blk", "tgt")),
        P(("blk", "tgt")),
    )
    out_specs = (P(None, None, ("blk", "tgt")), P(None, ("blk", "tgt")))
    return jax.shard_map(
        on_device, mesh=mesh, in_specs=in_specs, out_specs=out_specs, check_vma=False
    )
```

profile of v0, /device:TPU:32, one launch (start us, length us, event | category | flops | bytes accessed | tf_op | source)
XLA Modules:
  0.0 295.5 jit_solution(2415706052495670528)
XLA Ops:
  7.2 0.0 copy-start
  7.2 0.0 all-gather.2.cloned.1.call-start
  7.2 1.7 convert_element_type.6
  8.9 0.0 all-gather.2.cloned.1.call-update
  8.9 0.7 copy.26
  9.7 0.1 reduce-window.8
  9.7 0.1 reduce
  9.9 0.1 convert_reduce_fusion
  10.0 0.6 dynamic_slice.10
  12.2 0.0 copy-done
  12.3 0.8 gather_fusion
  13.1 135.9 %all-gather.2.cloned.1.call-done = bf16[4096,1536]{1,0:T(8,128)(2,1)} async-done(((bf16[64,1536]{1,0:T(8,128)(2,1)}), bf16[4096,1536]{1,0:T(8,128)(2,1)}) %all-gather.2.cloned.1.call-update) | async-done | bytes 12582928 | tf_op jit(solution)/shard_map/all_gather | solution.py:43
  149.0 35.0 %copy.27 = bf16[64,64,1536]{1,0,2:T(8,128)(2,1)} copy(bf16[64,64,1536]{2,1,0:T(8,128)(2,1)} %bitcast.39) | data formatting | bytes 25165824 | tf_op jit(solution)/shard_map/reshape | solution.py:45
  184.0 24.2 %gather_fusion.1 = bf16[64,64,384]{1,0,2:T(8,128)(2,1)} fusion(bf16[64,64,1536]{1,0,2:T(8,128)(2,1)} %copy.27, s32[64]{0:T(128)S(1)} %or_bitcast_fusion), kind=kCustom, calls=%fused_computation.1 | custom fusion | bytes 6292224 | tf_op jit(solution)/shard_map/vmap()/gather | solution.py:40
  208.1 0.0 copy-start.2
  208.2 0.0 copy-start.3
  208.2 0.0 copy-start.4
  208.2 12.3 %fusion.4 = f32[384,512,1]{0,1,2:T(8,128)} fusion(bf16[64,64,512]{2,1,0:T(8,128)(2,1)} %param.10, bf16[64,64,384]{1,0,2:T(8,128)(2,1)} %gather_fusion.1), kind=kOutput, calls=%fused_computation.8 | convolution fusion | flops 1610612736 | bytes 8126464 | tf_op jit(solution)/shard_map/gyw,gyt->wt/dot_general | solution.py:47
  220.5 10.0 %all-to-all-start = ((f32[8,384,64]{1,2,0:T(8,128)}), f32[8,384,64]{1,2,0:T(8,128)S(1)}, u32[]{:S(2)}, u32[]{:S(2)}) async-start(f32[8,384,64]{1,2,0:T(8,128)} %bitcast.13), calls=%async_computation | async-start | bytes 1572864 | tf_op jit(solution)/shard_map/all_to_all | solution.py:17
  230.5 47.3 %all-to-all-done = f32[8,384,64]{1,2,0:T(8,128)S(1)} async-done(((f32[8,384,64]{1,2,0:T(8,128)}), f32[8,384,64]{1,2,0:T(8,128)S(1)}, u32[]{:S(2)}, u32[]{:S(2)}) %all-to-all-start) | async-done | bytes 786464 | tf_op jit(solution)/shard_map/all_to_all | solution.py:17
  277.9 0.1 copy.30
  278.0 0.0 copy-done.2
  278.0 0.0 copy-done.3
  278.1 0.0 copy-done.4
  278.1 10.0 %while.12 = (s32[]{:T(128)}, f32[24,64]{1,0:T(8,128)S(1)}, f32[16,24,64]{2,1,0:T(8,128)}, f32[64]{0:T(128)S(1)}, f32[64]{0:T(128)S(1)}, /*index=5*/f32[16,24,64]{2,1,0:T(8,128)S(1)}, s32[]{:T(128)}) while((s32[]{:T(128)}, f32[24,64]{1,0:T(8,128)S(1)}, f32[16,24,64]{2,1,0:T(8,128)}, f32[64]{0:T(128)S(1)}, f32[64]{0:T(128)S(1)}, ...), condition=%wide.region_4.5_spmd, body=%wide.region_3.4_spmd.sunk | while | flops 15362 | bytes 31821 | solution.py:57
  278.1 0.6 fusion.11
  278.7 0.6 fusion.11
  279.3 0.6 fusion.11
  280.0 0.6 fusion.11
  280.6 0.6 fusion.11
  281.2 0.6 fusion.11
  281.8 0.6 fusion.11
  282.5 0.6 fusion.11
  283.1 0.6 fusion.11
  283.7 0.6 fusion.11
  284.3 0.6 fusion.11
  285.0 0.6 fusion.11
  285.6 0.6 fusion.11
  286.2 0.6 fusion.11
  286.8 0.6 fusion.11
  287.4 0.6 fusion.11
  288.1 0.0 copy-start.1
  288.1 0.6 copy-done.1
  (6 shorter events, 0.1 us)
Async XLA Ops:
  7.2 5.1 %copy-start = (s32[32,32]{1,0:T(8,128)S(1)}, s32[32,32]{1,0:T(8,128)}, u32[]{:S(2)}) copy-start(s32[32,32]{1,0:T(8,128)} %param.11) | copy-start | bytes 12292
  7.2 141.8 %all-gather.2.cloned.1.call-start = ((), (), s32[]{:S(2)}) async-start(), calls=%async_computation.1 | async-start | bytes 12779520 | tf_op jit(solution)/shard_map/all_gather | solution.py:43
  208.1 69.9 %copy-start.2 = (f32[24,64]{1,0:T(8,128)S(1)}, f32[24,64]{1,0:T(8,128)}, u32[]{:S(2)}) copy-start(f32[24,64]{1,0:T(8,128)} %param.13) | copy-start | bytes 18436
  208.2 69.9 %copy-start.3 = (f32[64]{0:T(128)S(1)}, f32[64]{0:T(128)}, u32[]{:S(2)}) copy-start(f32[64]{0:T(128)} %param.14) | copy-start | bytes 772
  208.2 69.9 %copy-start.4 = (f32[64]{0:T(128)S(1)}, f32[64]{0:T(128)}, u32[]{:S(2)}) copy-start(f32[64]{0:T(128)} %param.15) | copy-start | bytes 772
  220.5 57.4 %all-to-all-start = ((f32[8,384,64]{1,2,0:T(8,128)}), f32[8,384,64]{1,2,0:T(8,128)S(1)}, u32[]{:S(2)}, u32[]{:S(2)}) async-start(f32[8,384,64]{1,2,0:T(8,128)} %bitcast.13), calls=%async_computation | async-start | bytes 1572864 | tf_op jit(solution)/shard_map/all_to_all | solution.py:17
  288.1 0.6 copy-start.1
Sparse Core Ops, SparseCore 0:
  10.7 138.2 all-gather.1
where the time goes:
time: 297 us; the launch traced here: 296 us
  waiting for transfers between devices  183 us (62%)
  local copies, waits for them, and re-layouts  62 us (21%)
  between operations  15.8 us (5%)
  matrix products  12.3 us (4%)
  other arithmetic  12 us (4%)
  starting transfers between devices  10.1 us (3%)
    all_gather x1, waiting for transfers between devices, on_device(): arrived = lax.all_gather(history_low, 'blk', axis=0, tiled=True)  136 us
    all_to_all x1, waiting for transfers between devices, summed_on_arrival(): lax.all_to_all(parts, axis, split_axis=0, concat_axis=0, tiled=True)  47.3 us
    reshape x1, local copies, waits for them, and re-layouts, on_device(): shaped = arrived.reshape(shard_count, piece_width, columns)  35 us
    gather x1, local copies, waits for them, and re-layouts, window(): return lax.dynamic_slice_in_dim(column, start, window_width, 1)  24.2 us
    dot_general x1, matrix products, on_device(): jnp.einsum('gyw,gyt->wt', delayed_input, weights, preferred_element_type=...  12.3 us
    all_to_all x1, starting transfers between devices, summed_on_arrival(): lax.all_to_all(parts, axis, split_axis=0, concat_axis=0, tiled=True)  10 us
    dynamic_update_slice x16, other arithmetic, on_device(): last_potential, rate_steps = lax.scan(advance, potential, own_input)  9.98 us
  transfers between devices with their start and end apart: 2, of which 2 were waited for; matrix products, arithmetic and copies ran while one was open for 1% of the time, Pallas kernels for 0%

commit v1 on v0

v1 whole, which is shorter than its diff:
```python
import functools

import jax
import jax.numpy as jnp
from jax import lax
from jax.experimental import pallas as pl
from jax.experimental.pallas import tpu as pltpu
from jax.sharding import PartitionSpec as P

MESH = pl.DeviceIdType.MESH
STEPS = 16
TRIALS = 24
GROUP = 8
PASSES = TRIALS // GROUP
HIST = 64
SPANS = HIST // STEPS
SHARE = 64
CHAIN = 8
RING = 4
PEERS = 8
AREAS = 32
LANES = STEPS * GROUP
OFFSET = 3
LAG = 3


def kernel(
    hist_ref, weights_hbm, delays_ref, blocks_ref, pot_ref, leak_ref, drive_ref,
    rates_ref, last_ref,
    weights, hbuf, spans, sent, got, acc, xgot, zsend, zgot, src_area, tgt_area,
    w_sem, zsend_sem, zrecv_sem, ysend_sem, yrecv_sem, xsend_sem, xrecv_sem, hsend_sem, hrecv_sem,
):
    blk = lax.axis_index("blk")
    tgt = lax.axis_index("tgt")
    core = lax.rem(blk, 2)
    z = lax.rem(blk // 2, CHAIN)
    y = blk // (2 * CHAIN)
    x = tgt // 2
    z_hi = lax.rem(tgt, 2)

    def block_at(yy, zz, cc):
        return (yy * CHAIN + zz) * 2 + cc

    def peer_block(k, zz):
        dy, dc = k // 2, k % 2
        return block_at(lax.rem(y + dy, RING), zz, lax.rem(core + dc, 2))

    def x_peer(dx):
        return (blk, lax.rem(x + dx, RING) * 2 + z_hi)

    across = (blk, x * 2 + 1 - z_hi)
    right = (block_at(y, z + 1, core), tgt)
    left = (block_at(y, z - 1, core), tgt)

    barrier = pltpu.get_barrier_semaphore()
    for k in range(1, PEERS):
        pl.semaphore_signal(barrier, 1, device_id=(peer_block(k, z), tgt), device_id_type=MESH)
    for dx in range(1, RING):
        pl.semaphore_signal(barrier, 1, device_id=x_peer(dx), device_id_type=MESH)
    pl.semaphore_signal(barrier, 1, device_id=across, device_id_type=MESH)

    @pl.when(z < CHAIN - 1)
    def _():
        pl.semaphore_signal(barrier, 1, device_id=right, device_id_type=MESH)

    @pl.when(z > 0)
    def _():
        pl.semaphore_signal(barrier, 1, device_id=left, device_id_type=MESH)

    w_copy = pltpu.make_async_copy(weights_hbm, weights, w_sem)
    w_copy.start()

    width = STEPS * TRIALS
    row = lax.broadcasted_iota(jnp.int32, (width, width), 0)
    col = lax.broadcasted_iota(jnp.int32, (width, width), 1)
    inner = lax.rem(col, LANES)
    wanted = (inner // GROUP) * TRIALS + (col // LANES) * GROUP + lax.rem(inner, GROUP)
    regroup = jnp.where(row == wanted, 1.0, 0.0).astype(jnp.bfloat16)
    for q in range(SPANS):
        part = hist_ref[:, q * width : (q + 1) * width].astype(jnp.bfloat16)
        moved = jnp.dot(part, regroup, preferred_element_type=jnp.float32).astype(jnp.bfloat16)
        for c in range(PASSES):
            hbuf[c, 0, q] = moved[:, c * LANES : (c + 1) * LANES]
    acc[...] = jnp.zeros_like(acc)

    sources = [block_at(y, zz, core) for zz in range(CHAIN)]
    targets = [peer_block(k, z) for k in range(PEERS)]

    def count(a, carry):
        edge, counts = carry[0] + blocks_ref[a], carry[1:]
        more = [n + jnp.where(edge <= b, 1, 0) for n, b in zip(counts, sources + targets)]
        return (edge, *more)

    counted = lax.fori_loop(0, AREAS, count, (jnp.int32(0),) * (1 + CHAIN + PEERS))[1:]
    for i in range(CHAIN):
        src_area[i] = jnp.minimum(counted[i], AREAS - 1)
    for i in range(PEERS):
        tgt_area[i] = jnp.minimum(counted[CHAIN + i], AREAS - 1)

    pl.semaphore_wait(
        barrier, PEERS - 1 + RING - 1 + 1 + jnp.where(z < CHAIN - 1, 1, 0) + jnp.where(z > 0, 1, 0)
    )

    def source_of(t):
        both = jnp.minimum(z, CHAIN - 1 - z)
        dist = jnp.where(t <= 2 * both, (t + 1) // 2, t - both)
        from_left = jnp.where(t <= 2 * both, lax.rem(t, 2), jnp.where(z >= CHAIN // 2, 1, 0))
        return jnp.where(from_left == 1, z - dist, z + dist)

    def slot_at(zr, zs):
        both = jnp.minimum(zr, CHAIN - 1 - zr)
        dist = jnp.abs(zr - zs)
        return jnp.where(dist <= both, 2 * dist - jnp.where(zs < zr, 1, 0), dist + both)

    def chain_copy(c, t, zs, to_right):
        there = slot_at(z + 1 if to_right else z - 1, zs)
        return pltpu.make_async_remote_copy(
            src_ref=hbuf.at[c, t],
            dst_ref=hbuf.at[c, there],
            send_sem=zsend_sem.at[1 if to_right else 0, c, t],
            recv_sem=zrecv_sem.at[c, there],
            device_id=right if to_right else left,
            device_id_type=MESH,
        )

    def chain_arrival(c, t):
        return pltpu.make_async_remote_copy(
            src_ref=hbuf.at[c, t],
            dst_ref=hbuf.at[c, t],
            send_sem=zsend_sem.at[0, c, t],
            recv_sem=zrecv_sem.at[c, t],
            device_id=left,
            device_id_type=MESH,
        )

    def goes_right(zs):
        return jnp.logical_and(zs <= z, z < CHAIN - 1)

    def goes_left(zs):
        return jnp.logical_and(zs >= z, z > 0)

    lane = lax.broadcasted_iota(jnp.int32, (SHARE, LANES), 1)

    def spread(c, t):
        @pl.when(t > 0)
        def _():
            chain_arrival(c, t).wait_recv()

        zs = source_of(t)

        @pl.when(goes_right(zs))
        def _():
            chain_copy(c, t, zs, True).start()

        @pl.when(goes_left(zs))
        def _():
            chain_copy(c, t, zs, False).start()

        for q in range(SPANS):
            spans[q] = hbuf[c, t, q].astype(jnp.float32)
        area = src_area[zs]
        for k in [1, 2, 3, 6, 7, 4, 5, 0]:
            begin = jnp.clip(HIST - delays_ref[tgt_area[k], area], 0, HIST - STEPS)
            span = begin // STEPS
            skip = lax.rem(begin, STEPS) * GROUP
            turn = lax.rem(LANES - skip, LANES)
            first = pltpu.roll(spans[span], turn, 1)
            second = pltpu.roll(spans[jnp.minimum(span + 1, SPANS - 1)], turn, 1)
            window = jnp.where(lane < LANES - skip, first, second).astype(jnp.bfloat16)
            if k == 0:
                got[c, t, 0] = window
            else:
                sent[c, t, k - 1] = window
                back = (RING - k // 2) % RING * 2 + k % 2
                pltpu.make_async_remote_copy(
                    src_ref=sent.at[c, t, k - 1],
                    dst_ref=got.at[c, t, back],
                    send_sem=ysend_sem.at[c, t],
                    recv_sem=yrecv_sem.at[c, t],
                    device_id=(peer_block(k, z), tgt),
                    device_id_type=MESH,
                ).start()

    def windows_copy(c, t):
        return pltpu.make_async_remote_copy(
            src_ref=sent.at[c, t],
            dst_ref=got.at[c, t, pl.ds(1, PEERS - 1)],
            send_sem=ysend_sem.at[c, t],
            recv_sem=yrecv_sem.at[c, t],
            device_id=(peer_block(1, z), tgt),
            device_id_type=MESH,
        )

    def product(c, t):
        windows_copy(c, t).wait_recv()
        zs = source_of(t)
        rows = got[c, t].reshape(PEERS * SHARE, LANES)
        columns = jnp.concatenate([weights[peer_block(k, zs)] for k in range(PEERS)], axis=0)
        sums = lax.dot_general(
            rows, columns, (((0,), (0,)), ((), ())), preferred_element_type=jnp.float32
        )
        for i in range(RING):
            acc[c, i] += sums[:, i * 2 * SHARE : (i + 1) * 2 * SHARE]

    def x_copy(c, dx):
        return pltpu.make_async_remote_copy(
            src_ref=acc.at[c, lax.rem(x + dx, RING)],
            dst_ref=xgot.at[c, RING - 1 - dx],
            send_sem=xsend_sem.at[c],
            recv_sem=xrecv_sem.at[c],
            device_id=x_peer(dx),
            device_id_type=MESH,
        )

    def x_all(c):
        return pltpu.make_async_remote_copy(
            src_ref=acc.at[c, pl.ds(0, RING - 1)],
            dst_ref=xgot.at[c],
            send_sem=xsend_sem.at[c],
            recv_sem=xrecv_sem.at[c],
            device_id=x_peer(1),
            device_id_type=MESH,
        )

    def z_copy(c):
        return pltpu.make_async_remote_copy(
            src_ref=zsend.at[c, 0],
            dst_ref=zgot.at[c],
            send_sem=hsend_sem.at[c],
            recv_sem=hrecv_sem.at[c],
            device_id=across,
            device_id_type=MESH,
        )

    def sum_x(c):
        x_all(c).wait_recv()
        total = acc[c, x] + xgot[c, 0] + xgot[c, 1] + xgot[c, 2]
        early, late = total[: LANES // 2], total[LANES // 2 :]
        share0 = jnp.where(lane < SHARE, early, pltpu.roll(late, SHARE, 1))
        share1 = jnp.where(lane < SHARE, pltpu.roll(early, SHARE, 1), late)
        zsend[c, z_hi] = share1
        zsend[c, 1 - z_hi] = share0
        z_copy(c).start()

    def integrate(c):
        z_copy(c).wait_recv()
        total = zsend[c, 1] + zgot[c]
        turned = pltpu.roll(total, SHARE, 1)
        mine = pl.ds(pl.multiple_of(c * GROUP, GROUP), GROUP)
        membrane = pot_ref[mine, :]
        leak, drive = leak_ref[...], drive_ref[...]
        for s in range(STEPS):
            half = total if s < STEPS // 2 else turned
            begin = s % (STEPS // 2) * GROUP
            synaptic = half[begin : begin + GROUP, :SHARE]
            membrane = membrane + leak * (drive - membrane + synaptic)
            rates_ref[s, mine, :] = jnp.maximum(membrane, 0.0) + jnp.log1p(jnp.exp(-jnp.abs(membrane)))
        last_ref[mine, :] = membrane

    w_copy.wait()

    def slot(k, _):
        def one(c, _):
            t = k - OFFSET * c

            @pl.when(jnp.logical_and(t >= 0, t < CHAIN))
            def _():
                spread(c, t)

            return 0

        def two(c, _):
            t = k - OFFSET * c - LAG

            @pl.when(jnp.logical_and(t >= 0, t < CHAIN))
            def _():
                product(c, t)

            @pl.when(t == CHAIN - 1)
            def _():
                for dx in range(1, RING):
                    x_copy(c, dx).start()

            return 0

        def three(c, _):
            t = k - OFFSET * c - LAG

            @pl.when(t == CHAIN)
            def _():
                sum_x(c)

            @pl.when(t == CHAIN + 1)
            def _():
                integrate(c)

            return 0

        lax.fori_loop(0, PASSES, one, 0)
        lax.fori_loop(0, PASSES, three, 0)
        lax.fori_loop(0, PASSES, two, 0)
        return 0

    lax.fori_loop(0, OFFSET * (PASSES - 1) + CHAIN + LAG + 2, slot, 0)

    def drain(n, _):
        c, t = n // CHAIN, lax.rem(n, CHAIN)
        zs = source_of(t)

        @pl.when(goes_right(zs))
        def _():
            chain_copy(c, t, zs, True).wait_send()

        @pl.when(goes_left(zs))
        def _():
            chain_copy(c, t, zs, False).wait_send()

        windows_copy(c, t).wait_send()

        @pl.when(t == 0)
        def _():
            x_all(c).wait_send()
            z_copy(c).wait_send()

        return 0

    lax.fori_loop(0, PASSES * CHAIN, drain, 0)


def on_device(history, weights, delays, area_blocks, potential, leak, drive):
    vmem = pl.BlockSpec(memory_space=pltpu.VMEM)
    smem = pl.BlockSpec(memory_space=pltpu.SMEM)
    dma = pltpu.SemaphoreType.DMA
    bf16, f32 = jnp.bfloat16, jnp.float32
    return pl.pallas_call(
        kernel,
        out_shape=(
            jax.ShapeDtypeStruct((STEPS, TRIALS, SHARE), f32),
            jax.ShapeDtypeStruct((TRIALS, SHARE), f32),
        ),
        in_specs=[vmem, pl.BlockSpec(memory_space=pl.ANY), smem, smem, vmem, vmem, vmem],
        out_specs=(vmem, vmem),
        scratch_shapes=[
            pltpu.VMEM(weights.shape, bf16),
            pltpu.VMEM((PASSES, CHAIN, SPANS, SHARE, LANES), bf16),
            pltpu.VMEM((SPANS, SHARE, LANES), f32),
            pltpu.VMEM((PASSES, CHAIN, PEERS - 1, SHARE, LANES), bf16),
            pltpu.VMEM((PASSES, CHAIN, PEERS, SHARE, LANES), bf16),
            pltpu.VMEM((PASSES, RING, LANES, 2 * SHARE), f32),
            pltpu.VMEM((PASSES, RING - 1, LANES, 2 * SHARE), f32),
            pltpu.VMEM((PASSES, 2, LANES // 2, 2 * SHARE), f32),
            pltpu.VMEM((PASSES, LANES // 2, 2 * SHARE), f32),
            pltpu.SMEM((CHAIN,), jnp.int32),
            pltpu.SMEM((PEERS,), jnp.int32),
            dma,
            dma((2, PASSES, CHAIN)),
            dma((PASSES, CHAIN)),
            dma((PASSES, CHAIN)),
            dma((PASSES, CHAIN)),
            dma((PASSES,)),
            dma((PASSES,)),
            dma((PASSES,)),
            dma((PASSES,)),
        ],
        compiler_params=pltpu.CompilerParams(
            collective_id=0, has_side_effects=True, vmem_limit_bytes=40 * 2**20
        ),
        name="network_interval",
    )(history, weights, delays, area_blocks, potential, leak.reshape(1, -1), drive.reshape(1, -1))


def solution(mesh):
    in_specs = (
        P(("blk", "tgt"), None),
        P(None, "tgt", "blk"),
        P(),
        P(),
        P(None, ("blk", "tgt")),
        P(("blk", "tgt")),
        P(("blk", "tgt")),
    )
    out_specs = (P(None, None, ("blk", "tgt")), P(None, ("blk", "tgt")))
    return jax.shard_map(
        on_device, mesh=mesh, in_specs=in_specs, out_specs=out_specs, check_vma=False
    )
```

time: 297 us -> 108 us (0.36)
  the two profiles are of different devices: /device:TPU:32 before, /device:TPU:24 now
where the time goes in v1:
time: 108 us; the launch traced here: 107 us
  Pallas kernels  98.2 us (91%)
  local copies, waits for them, and re-layouts  7.84 us (7%)
    pallas_call x1, Pallas kernels, on_device(): pl.pallas_call(kernel, out_shape=(jax.ShapeDtypeStruct((STEPS, TRIALS, SH...  98.2 us
    unnamed x16, local copies, waits for them, and re-layouts  7.84 us

profile of v1, /device:TPU:24, one launch (start us, length us, event | category | flops | bytes accessed | tf_op | source)
XLA Modules:
  0.0 106.7 jit_solution(7981149549243010839)
XLA Ops:
  0.6 0.0 copy-start
  0.6 2.2 %copy-done = bf16[64,64,512]{2,1,0:T(8,128)(2,1)S(1)} copy-done((bf16[64,64,512]{2,1,0:T(8,128)(2,1)S(1)}, bf16[64,64,512]{2,1,0:T(8,128)(2,1)}, u32[]{:S(2)}) %copy-start) | copy-done | bytes 4194328
  2.8 0.0 copy-start.1
  2.8 1.0 copy-done.1
  3.8 0.0 copy-start.2
  3.8 0.7 copy-done.2
  4.5 0.0 copy-start.3
  4.5 0.7 copy-done.3
  5.2 0.0 copy-start.4
  5.2 0.7 copy-done.4
  5.9 0.0 copy-start.5
  5.9 0.7 copy-done.5
  6.6 0.0 copy-start.6
  6.6 0.7 copy-done.6
  7.2 98.2 %network_interval.1 = (f32[16,24,64]{2,1,0:T(8,128)S(1)}, f32[24,64]{1,0:T(8,128)S(1)}) custom-call(f32[64,1536]{1,0:T(8,128)S(1)} %copy-done.1, bf16[64,64,512]{2,1,0:T(8,128)(2,1)S(1)} %copy-done, s32[32,32]{1,0:T(8,128)S(1)} %copy-done.2, s32[32]{0:T(128)S(1)} %copy-done.4, f32[24,64]{1,0:T(8,128)S(1)} %copy-done.3, f32[1,64]{1,0:T(1,128)S(1)} %bitcast.2, ...), custom_call_target="tpu_custom_call" | custom-call | tf_op jit(solution)/shard_map/network_interval/pallas_call | solution.py:335
  105.4 0.7 copy.11
  106.1 0.6 copy.12
Async XLA Ops:
  0.6 2.2 %copy-start = (bf16[64,64,512]{2,1,0:T(8,128)(2,1)S(1)}, bf16[64,64,512]{2,1,0:T(8,128)(2,1)}, u32[]{:S(2)}) copy-start(bf16[64,64,512]{2,1,0:T(8,128)(2,1)} %weights_hbm.1) | copy-start | bytes 12582916
  2.8 1.0 copy-start.1
  3.8 0.7 copy-start.2
  4.5 0.7 copy-start.3
  5.2 0.7 copy-start.4
  5.9 0.7 copy-start.5
  6.6 0.7 copy-start.6

commit v2 on v1

--- a/solution.py
+++ b/solution.py
@@ -20,15 +20,15 @@
 PEERS = 8
 AREAS = 32
 LANES = STEPS * GROUP
-OFFSET = 3
-LAG = 3
+OFFSET = 0
+LAG = 2
 
 
 def kernel(
-    hist_ref, weights_hbm, delays_ref, blocks_ref, pot_ref, leak_ref, drive_ref,
+    hist_hbm, weights_hbm, delays_hbm, blocks_hbm, pot_hbm, leak_hbm, drive_hbm,
     rates_ref, last_ref,
-    weights, hbuf, spans, sent, got, acc, xgot, zsend, zgot, src_area, tgt_area,
-    w_sem, zsend_sem, zrecv_sem, ysend_sem, yrecv_sem, xsend_sem, xrecv_sem, hsend_sem, hrecv_sem,
+    hist_ref, weights, delays_ref, blocks_ref, pot_ref, leak_ref, drive_ref, hbuf, spans, sent, got, acc, xgot, zsend, zgot, src_area, tgt_area,
+    in_sem, zsend_sem, zrecv_sem, ysend_sem, yrecv_sem, xsend_sem, xrecv_sem, hsend_sem, hrecv_sem,
 ):
     blk = lax.axis_index("blk")
     tgt = lax.axis_index("tgt")
@@ -52,6 +52,14 @@
     right = (block_at(y, z + 1, core), tgt)
     left = (block_at(y, z - 1, core), tgt)
 
+    pairs = [
+        (hist_hbm, hist_ref), (blocks_hbm, blocks_ref), (delays_hbm, delays_ref), (weights_hbm, weights),
+        (pot_hbm, pot_ref), (leak_hbm, leak_ref), (drive_hbm, drive_ref),
+    ]
+    loads = [pltpu.make_async_copy(a, b, in_sem.at[i]) for i, (a, b) in enumerate(pairs)]
+    for load in loads:
+        load.start()
+
     barrier = pltpu.get_barrier_semaphore()
     for k in range(1, PEERS):
         pl.semaphore_signal(barrier, 1, device_id=(peer_block(k, z), tgt), device_id_type=MESH)
@@ -67,15 +75,13 @@
     def _():
         pl.semaphore_signal(barrier, 1, device_id=left, device_id_type=MESH)
 
-    w_copy = pltpu.make_async_copy(weights_hbm, weights, w_sem)
-    w_copy.start()
-
     width = STEPS * TRIALS
     row = lax.broadcasted_iota(jnp.int32, (width, width), 0)
     col = lax.broadcasted_iota(jnp.int32, (width, width), 1)
     inner = lax.rem(col, LANES)
     wanted = (inner // GROUP) * TRIALS + (col // LANES) * GROUP + lax.rem(inner, GROUP)
     regroup = jnp.where(row == wanted, 1.0, 0.0).astype(jnp.bfloat16)
+    loads[0].wait()
     for q in range(SPANS):
         part = hist_ref[:, q * width : (q + 1) * width].astype(jnp.bfloat16)
         moved = jnp.dot(part, regroup, preferred_element_type=jnp.float32).astype(jnp.bfloat16)
@@ -91,6 +97,7 @@
         more = [n + jnp.where(edge <= b, 1, 0) for n, b in zip(counts, sources + targets)]
         return (edge, *more)
 
+    loads[1].wait()
     counted = lax.fori_loop(0, AREAS, count, (jnp.int32(0),) * (1 + CHAIN + PEERS))[1:]
     for i in range(CHAIN):
         src_area[i] = jnp.minimum(counted[i], AREAS - 1)
@@ -257,7 +264,8 @@
             rates_ref[s, mine, :] = jnp.maximum(membrane, 0.0) + jnp.log1p(jnp.exp(-jnp.abs(membrane)))
         last_ref[mine, :] = membrane
 
-    w_copy.wait()
+    for load in loads[2:]:
+        load.wait()
 
     def slot(k, _):
         def one(c, _):
@@ -329,7 +337,6 @@
 
 def on_device(history, weights, delays, area_blocks, potential, leak, drive):
     vmem = pl.BlockSpec(memory_space=pltpu.VMEM)
-    smem = pl.BlockSpec(memory_space=pltpu.SMEM)
     dma = pltpu.SemaphoreType.DMA
     bf16, f32 = jnp.bfloat16, jnp.float32
     return pl.pallas_call(
@@ -338,10 +345,16 @@
             jax.ShapeDtypeStruct((STEPS, TRIALS, SHARE), f32),
             jax.ShapeDtypeStruct((TRIALS, SHARE), f32),
         ),
-        in_specs=[vmem, pl.BlockSpec(memory_space=pl.ANY), smem, smem, vmem, vmem, vmem],
+        in_specs=[pl.BlockSpec(memory_space=pltpu.HBM)] * 7,
         out_specs=(vmem, vmem),
         scratch_shapes=[
+            pltpu.VMEM(history.shape, f32),
             pltpu.VMEM(weights.shape, bf16),
+            pltpu.SMEM(delays.shape, jnp.int32),
+            pltpu.SMEM(area_blocks.shape, jnp.int32),
+            pltpu.VMEM(potential.shape, f32),
+            pltpu.VMEM((1, SHARE), f32),
+            pltpu.VMEM((1, SHARE), f32),
             pltpu.VMEM((PASSES, CHAIN, SPANS, SHARE, LANES), bf16),
             pltpu.VMEM((SPANS, SHARE, LANES), f32),
             pltpu.VMEM((PASSES, CHAIN, PEERS - 1, SHARE, LANES), bf16),
@@ -352,7 +365,7 @@
             pltpu.VMEM((PASSES, LANES // 2, 2 * SHARE), f32),
             pltpu.SMEM((CHAIN,), jnp.int32),
             pltpu.SMEM((PEERS,), jnp.int32),
-            dma,
+            dma((7,)),
             dma((2, PASSES, CHAIN)),
             dma((PASSES, CHAIN)),
             dma((PASSES, CHAIN)),
@@ -363,7 +376,7 @@
             dma((PASSES,)),
         ],
         compiler_params=pltpu.CompilerParams(
-            collective_id=0, has_side_effects=True, vmem_limit_bytes=40 * 2**20
+            collective_id=0, has_side_effects=True, vmem_limit_bytes=56 * 2**20
         ),
         name="network_interval",
     )(history, weights, delays, area_blocks, potential, leak.reshape(1, -1), drive.reshape(1, -1))

time: 108 us -> 80.8 us (0.75)
  Pallas kernels: 98.2 us -> 76.5 us
  local copies, waits for them, and re-layouts: 7.84 us -> 2.92 us
    pallas_call x1, Pallas kernels: 98.2 us -> 76.5 us  [on_device(): pl.pallas_call(kernel, out_shape=(jax.ShapeDtypeStruct((STEPS, TRIALS, SH...]
    unnamed x16 -> x2, local copies, waits for them, and re-layouts: 7.84 us -> 2.92 us
where the time goes in v2:
time: 80.8 us; the launch traced here: 80.1 us
  Pallas kernels  76.5 us (95%)
  local copies, waits for them, and re-layouts  2.92 us (4%)
    pallas_call x1, Pallas kernels, on_device(): pl.pallas_call(kernel, out_shape=(jax.ShapeDtypeStruct((STEPS, TRIALS, SH...  76.5 us
    unnamed x2, local copies, waits for them, and re-layouts  2.92 us

profile of v2, /device:TPU:24, one launch (start us, length us, event | category | flops | bytes accessed | tf_op | source)
XLA Modules:
  0.0 80.1 jit_solution(3340887147548944248)
XLA Ops:
  0.6 76.5 %network_interval.1 = (f32[16,24,64]{2,1,0:T(8,128)}, f32[24,64]{1,0:T(8,128)}) custom-call(f32[64,1536]{1,0:T(8,128)} %hist_hbm.1, bf16[64,64,512]{2,1,0:T(8,128)(2,1)} %weights_hbm.1, s32[32,32]{1,0:T(8,128)} %delays_hbm.1, s32[32]{0:T(128)} %blocks_hbm.1, f32[24,64]{1,0:T(8,128)} %pot_hbm.1, f32[1,64]{1,0:T(1,128)} %bitcast.2, f32[1,64]{1,0:T(1,128)} %bitcast.3), custom_call_target="tpu_custom_call" | custom-call | tf_op jit(solution)/shard_map/network_interval/pallas_call | solution.py:342
  77.2 1.6 %copy.11 = f32[16,24,64]{2,1,0:T(8,128)} copy(f32[16,24,64]{2,1,0:T(8,128)} %get-tuple-element.4) | data formatting | bytes 196608
  78.8 1.3 %copy.12 = f32[24,64]{1,0:T(8,128)} copy(f32[24,64]{1,0:T(8,128)} %get-tuple-element.5) | data formatting | bytes 12288

commit v3 on v2

--- a/solution.py
+++ b/solution.py
@@ -21,7 +21,10 @@
 AREAS = 32
 LANES = STEPS * GROUP
 OFFSET = 0
-LAG = 2
+SPAN_TYPE = jnp.bfloat16
+ORDER = (4, 5, 2, 3, 6, 7, 1, 0)
+
+LAG = 3
 
 
 def kernel(
@@ -87,6 +90,62 @@
         moved = jnp.dot(part, regroup, preferred_element_type=jnp.float32).astype(jnp.bfloat16)
         for c in range(PASSES):
             hbuf[c, 0, q] = moved[:, c * LANES : (c + 1) * LANES]
+
+    pl.semaphore_wait(
+        barrier, PEERS - 1 + RING - 1 + 1 + jnp.where(z < CHAIN - 1, 1, 0) + jnp.where(z > 0, 1, 0)
+    )
+
+    def source_of(t):
+        both = jnp.minimum(z, CHAIN - 1 - z)
+        dist = jnp.where(t <= 2 * both, (t + 1) // 2, t - both)
+        from_left = jnp.where(t <= 2 * both, lax.rem(t, 2), jnp.where(z >= CHAIN // 2, 1, 0))
+        return jnp.where(from_left == 1, z - dist, z + dist)
+
+    def slot_at(zr, zs):
+        both = jnp.minimum(zr, CHAIN - 1 - zr)
+        dist = jnp.abs(zr - zs)
+        return jnp.where(dist <= both, 2 * dist - jnp.where(zs < zr, 1, 0), dist + both)
+
+    def chain_copy(c, t, zs, to_right):
+        there = slot_at(z + 1 if to_right else z - 1, zs)
+        return pltpu.make_async_remote_copy(
+            src_ref=hbuf.at[c, t],
+            dst_ref=hbuf.at[c, there],
+            send_sem=zsend_sem.at[1 if to_right else 0, c, t],
+            recv_sem=zrecv_sem.at[c, there],
+            device_id=right if to_right else left,
+            device_id_type=MESH,
+        )
+
+    def chain_arrival(c, t):
+        return pltpu.make_async_remote_copy(
+            src_ref=hbuf.at[c, t],
+            dst_ref=hbuf.at[c, t],
+            send_sem=zsend_sem.at[0, c, t],
+            recv_sem=zrecv_sem.at[c, t],
+            device_id=left,
+            device_id_type=MESH,
+        )
+
+    def goes_right(zs):
+        return jnp.logical_and(zs <= z, z < CHAIN - 1)
+
+    def goes_left(zs):
+        return jnp.logical_and(zs >= z, z > 0)
+
+    def pass_on(c, t):
+        zs = source_of(t)
+
+        @pl.when(goes_right(zs))
+        def _():
+            chain_copy(c, t, zs, True).start()
+
+        @pl.when(goes_left(zs))
+        def _():
+            chain_copy(c, t, zs, False).start()
+
+    for c in range(PASSES):
+        pass_on(c, 0)
     acc[...] = jnp.zeros_like(acc)
 
     sources = [block_at(y, zz, core) for zz in range(CHAIN)]
@@ -104,72 +163,23 @@
     for i in range(PEERS):
         tgt_area[i] = jnp.minimum(counted[CHAIN + i], AREAS - 1)
 
-    pl.semaphore_wait(
-        barrier, PEERS - 1 + RING - 1 + 1 + jnp.where(z < CHAIN - 1, 1, 0) + jnp.where(z > 0, 1, 0)
-    )
-
-    def source_of(t):
-        both = jnp.minimum(z, CHAIN - 1 - z)
-        dist = jnp.where(t <= 2 * both, (t + 1) // 2, t - both)
-        from_left = jnp.where(t <= 2 * both, lax.rem(t, 2), jnp.where(z >= CHAIN // 2, 1, 0))
-        return jnp.where(from_left == 1, z - dist, z + dist)
-
-    def slot_at(zr, zs):
-        both = jnp.minimum(zr, CHAIN - 1 - zr)
-        dist = jnp.abs(zr - zs)
-        return jnp.where(dist <= both, 2 * dist - jnp.where(zs < zr, 1, 0), dist + both)
-
-    def chain_copy(c, t, zs, to_right):
-        there = slot_at(z + 1 if to_right else z - 1, zs)
-        return pltpu.make_async_remote_copy(
-            src_ref=hbuf.at[c, t],
-            dst_ref=hbuf.at[c, there],
-            send_sem=zsend_sem.at[1 if to_right else 0, c, t],
-            recv_sem=zrecv_sem.at[c, there],
-            device_id=right if to_right else left,
-            device_id_type=MESH,
-        )
-
-    def chain_arrival(c, t):
-        return pltpu.make_async_remote_copy(
-            src_ref=hbuf.at[c, t],
-            dst_ref=hbuf.at[c, t],
-            send_sem=zsend_sem.at[0, c, t],
-            recv_sem=zrecv_sem.at[c, t],
-            device_id=left,
-            device_id_type=MESH,
-        )
-
-    def goes_right(zs):
-        return jnp.logical_and(zs <= z, z < CHAIN - 1)
-
-    def goes_left(zs):
-        return jnp.logical_and(zs >= z, z > 0)
-
     lane = lax.broadcasted_iota(jnp.int32, (SHARE, LANES), 1)
 
     def spread(c, t):
         @pl.when(t > 0)
         def _():
             chain_arrival(c, t).wait_recv()
-
-        zs = source_of(t)
-
-        @pl.when(goes_right(zs))
-        def _():
-            chain_copy(c, t, zs, True).start()
-
-        @pl.when(goes_left(zs))
-        def _():
-            chain_copy(c, t, zs, False).start()
-
+            pass_on(c, t)
+
+        area = src_area[source_of(t)]
+        begins = [
+            jnp.clip(HIST - delays_ref[tgt_area[k], area], 0, HIST - STEPS) for k in range(PEERS)
+        ]
         for q in range(SPANS):
-            spans[q] = hbuf[c, t, q].astype(jnp.float32)
-        area = src_area[zs]
-        for k in [1, 2, 3, 6, 7, 4, 5, 0]:
-            begin = jnp.clip(HIST - delays_ref[tgt_area[k], area], 0, HIST - STEPS)
-            span = begin // STEPS
-            skip = lax.rem(begin, STEPS) * GROUP
+            spans[q] = hbuf[c, t, q].astype(SPAN_TYPE)
+        for k in ORDER:
+            span = begins[k] // STEPS
+            skip = lax.rem(begins[k], STEPS) * GROUP
             turn = lax.rem(LANES - skip, LANES)
             first = pltpu.roll(spans[span], turn, 1)
             second = pltpu.roll(spans[jnp.minimum(span + 1, SPANS - 1)], turn, 1)
@@ -178,15 +188,16 @@
                 got[c, t, 0] = window
             else:
                 sent[c, t, k - 1] = window
-                back = (RING - k // 2) % RING * 2 + k % 2
-                pltpu.make_async_remote_copy(
-                    src_ref=sent.at[c, t, k - 1],
-                    dst_ref=got.at[c, t, back],
-                    send_sem=ysend_sem.at[c, t],
-                    recv_sem=yrecv_sem.at[c, t],
-                    device_id=(peer_block(k, z), tgt),
-                    device_id_type=MESH,
-                ).start()
+        for k in ORDER[:-1]:
+            back = (RING - k // 2) % RING * 2 + k % 2
+            pltpu.make_async_remote_copy(
+                src_ref=sent.at[c, t, k - 1],
+                dst_ref=got.at[c, t, back],
+                send_sem=ysend_sem.at[c, t],
+                recv_sem=yrecv_sem.at[c, t],
+                device_id=(peer_block(k, z), tgt),
+                device_id_type=MESH,
+            ).start()
 
     def windows_copy(c, t):
         return pltpu.make_async_remote_copy(
@@ -342,8 +353,8 @@
     return pl.pallas_call(
         kernel,
         out_shape=(
-            jax.ShapeDtypeStruct((STEPS, TRIALS, SHARE), f32),
-            jax.ShapeDtypeStruct((TRIALS, SHARE), f32),
+            pltpu.VMEM((STEPS, TRIALS, SHARE), f32),
+            pltpu.VMEM((TRIALS, SHARE), f32),
         ),
         in_specs=[pl.BlockSpec(memory_space=pltpu.HBM)] * 7,
         out_specs=(vmem, vmem),
@@ -356,7 +367,7 @@
             pltpu.VMEM((1, SHARE), f32),
             pltpu.VMEM((1, SHARE), f32),
             pltpu.VMEM((PASSES, CHAIN, SPANS, SHARE, LANES), bf16),
-            pltpu.VMEM((SPANS, SHARE, LANES), f32),
+            pltpu.VMEM((SPANS, SHARE, LANES), SPAN_TYPE),
             pltpu.VMEM((PASSES, CHAIN, PEERS - 1, SHARE, LANES), bf16),
             pltpu.VMEM((PASSES, CHAIN, PEERS, SHARE, LANES), bf16),
             pltpu.VMEM((PASSES, RING, LANES, 2 * SHARE), f32),

time: 80.8 us -> 74.9 us (0.927)
  Pallas kernels: 76.5 us -> 72.8 us
  local copies, waits for them, and re-layouts: 2.92 us -> 1.28 us
    pallas_call x1, Pallas kernels: 76.5 us -> 72.8 us  [on_device(): pl.pallas_call(kernel, out_shape=(pltpu.VMEM((STEPS, TRIALS, SHARE), f32)...]
    unnamed x2, local copies, waits for them, and re-layouts: 2.92 us -> 1.28 us
where the time goes in v3:
time: 74.9 us; the launch traced here: 74.7 us
  Pallas kernels  72.8 us (97%)
  local copies, waits for them, and re-layouts  1.28 us (2%)
    pallas_call x1, Pallas kernels, on_device(): pl.pallas_call(kernel, out_shape=(pltpu.VMEM((STEPS, TRIALS, SHARE), f32)...  72.8 us

profile of v3, /device:TPU:24, one launch (start us, length us, event | category | flops | bytes accessed | tf_op | source)
XLA Modules:
  0.0 74.7 jit_solution(6790876969109558260)
XLA Ops:
  0.6 72.8 %network_interval.1 = (f32[16,24,64]{2,1,0:T(8,128)S(1)}, f32[24,64]{1,0:T(8,128)S(1)}) custom-call(f32[64,1536]{1,0:T(8,128)} %hist_hbm.1, bf16[64,64,512]{2,1,0:T(8,128)(2,1)} %weights_hbm.1, s32[32,32]{1,0:T(8,128)} %delays_hbm.1, s32[32]{0:T(128)} %blocks_hbm.1, f32[24,64]{1,0:T(8,128)} %pot_hbm.1, f32[1,64]{1,0:T(1,128)} %bitcast.2, f32[1,64]{1,0:T(1,128)} %bitcast.3), custom_call_target="tpu_custom_call" | custom-call | tf_op jit(solution)/shard_map/network_interval/pallas_call | solution.py:353
  73.5 0.7 copy.11
  74.1 0.6 copy.12

commit v4 on v3

--- a/solution.py
+++ b/solution.py
@@ -20,6 +20,10 @@
 PEERS = 8
 AREAS = 32
 LANES = STEPS * GROUP
+HEAD = 16
+CODE_MAX = 32767.0
+COARSE = 16.0
+FINE = 32768.0
 OFFSET = 0
 SPAN_TYPE = jnp.bfloat16
 ORDER = (4, 5, 2, 3, 6, 7, 1, 0)
@@ -30,7 +34,7 @@
 def kernel(
     hist_hbm, weights_hbm, delays_hbm, blocks_hbm, pot_hbm, leak_hbm, drive_hbm,
     rates_ref, last_ref,
-    hist_ref, weights, delays_ref, blocks_ref, pot_ref, leak_ref, drive_ref, hbuf, spans, sent, got, acc, xgot, zsend, zgot, src_area, tgt_area,
+    hist_ref, weights, delays_ref, blocks_ref, pot_ref, leak_ref, drive_ref, hbuf, spans, sent, got, acc, own, xsend, xgot, zsend, zgot, src_area, tgt_area,
     in_sem, zsend_sem, zrecv_sem, ysend_sem, yrecv_sem, xsend_sem, xrecv_sem, hsend_sem, hrecv_sem,
 ):
     blk = lax.axis_index("blk")
@@ -220,9 +224,35 @@
         for i in range(RING):
             acc[c, i] += sums[:, i * 2 * SHARE : (i + 1) * 2 * SHARE]
 
+    def encode(values):
+        top, low = jnp.max(values, axis=0, keepdims=True), jnp.min(values, axis=0, keepdims=True)
+
+        def split(v):
+            coarse = jnp.clip(jnp.round(v * COARSE), -CODE_MAX, CODE_MAX)
+            return coarse, jnp.clip(jnp.round((v * COARSE - coarse) * FINE), -CODE_MAX, CODE_MAX)
+
+        middle = split(0.5 * (top + low))
+        half = split(0.5 * (top - low) + 4.0 / (COARSE * FINE))
+        row = lax.broadcasted_iota(jnp.int32, (HEAD, values.shape[1]), 0)
+        head = jnp.zeros((HEAD, values.shape[1]), jnp.float32)
+        for i, part in enumerate(middle + half):
+            head = jnp.where(row == i, part, head)
+        body = jnp.round((values - joined(*middle)) * (CODE_MAX / joined(*half)))
+        codes = jnp.concatenate([jnp.clip(body, -CODE_MAX, CODE_MAX), head], axis=0)
+        return codes.astype(jnp.int32).astype(jnp.int16)
+
+    def joined(coarse, fine):
+        return coarse * (1.0 / COARSE) + fine * (1.0 / (COARSE * FINE))
+
+    def decode(codes):
+        numbers = codes.astype(jnp.int32).astype(jnp.float32)
+        rows = codes.shape[0] - HEAD
+        head = [numbers[rows + i : rows + i + 1] for i in range(4)]
+        return joined(*head[:2]) + numbers[:rows] * (joined(*head[2:]) * (1.0 / CODE_MAX))
+
     def x_copy(c, dx):
         return pltpu.make_async_remote_copy(
-            src_ref=acc.at[c, lax.rem(x + dx, RING)],
+            src_ref=xsend.at[c, dx - 1],
             dst_ref=xgot.at[c, RING - 1 - dx],
             send_sem=xsend_sem.at[c],
             recv_sem=xrecv_sem.at[c],
@@ -232,7 +262,7 @@
 
     def x_all(c):
         return pltpu.make_async_remote_copy(
-            src_ref=acc.at[c, pl.ds(0, RING - 1)],
+            src_ref=xsend.at[c],
             dst_ref=xgot.at[c],
             send_sem=xsend_sem.at[c],
             recv_sem=xrecv_sem.at[c],
@@ -240,9 +270,14 @@
             device_id_type=MESH,
         )
 
+    def send_x(c):
+        for dx in (2, 1, 3):
+            xsend[c, dx - 1] = encode(acc[c, lax.rem(x + dx, RING)])
+            x_copy(c, dx).start()
+
     def z_copy(c):
         return pltpu.make_async_remote_copy(
-            src_ref=zsend.at[c, 0],
+            src_ref=zsend.at[c],
             dst_ref=zgot.at[c],
             send_sem=hsend_sem.at[c],
             recv_sem=hrecv_sem.at[c],
@@ -252,17 +287,18 @@
 
     def sum_x(c):
         x_all(c).wait_recv()
-        total = acc[c, x] + xgot[c, 0] + xgot[c, 1] + xgot[c, 2]
+        total = acc[c, x] + decode(xgot[c, 0]) + decode(xgot[c, 1]) + decode(xgot[c, 2])
         early, late = total[: LANES // 2], total[LANES // 2 :]
         share0 = jnp.where(lane < SHARE, early, pltpu.roll(late, SHARE, 1))
         share1 = jnp.where(lane < SHARE, pltpu.roll(early, SHARE, 1), late)
-        zsend[c, z_hi] = share1
-        zsend[c, 1 - z_hi] = share0
+        first = z_hi == 0
+        zsend[c] = encode(jnp.where(first, share1, share0))
         z_copy(c).start()
+        own[c] = jnp.where(first, share0, share1)
 
     def integrate(c):
         z_copy(c).wait_recv()
-        total = zsend[c, 1] + zgot[c]
+        total = own[c] + decode(zgot[c])
         turned = pltpu.roll(total, SHARE, 1)
         mine = pl.ds(pl.multiple_of(c * GROUP, GROUP), GROUP)
         membrane = pot_ref[mine, :]
@@ -297,8 +333,7 @@
 
             @pl.when(t == CHAIN - 1)
             def _():
-                for dx in range(1, RING):
-                    x_copy(c, dx).start()
+                send_x(c)
 
             return 0
 
@@ -371,9 +406,11 @@
             pltpu.VMEM((PASSES, CHAIN, PEERS - 1, SHARE, LANES), bf16),
             pltpu.VMEM((PASSES, CHAIN, PEERS, SHARE, LANES), bf16),
             pltpu.VMEM((PASSES, RING, LANES, 2 * SHARE), f32),
-            pltpu.VMEM((PASSES, RING - 1, LANES, 2 * SHARE), f32),
-            pltpu.VMEM((PASSES, 2, LANES // 2, 2 * SHARE), f32),
             pltpu.VMEM((PASSES, LANES // 2, 2 * SHARE), f32),
+            pltpu.VMEM((PASSES, RING - 1, LANES + HEAD, 2 * SHARE), jnp.int16),
+            pltpu.VMEM((PASSES, RING - 1, LANES + HEAD, 2 * SHARE), jnp.int16),
+            pltpu.VMEM((PASSES, LANES // 2 + HEAD, 2 * SHARE), jnp.int16),
+            pltpu.VMEM((PASSES, LANES // 2 + HEAD, 2 * SHARE), jnp.int16),
             pltpu.SMEM((CHAIN,), jnp.int32),
             pltpu.SMEM((PEERS,), jnp.int32),
             dma((7,)),

time: 74.9 us -> 69.3 us (0.925)
  Pallas kernels: 72.8 us -> 67 us
    pallas_call x1, Pallas kernels: 72.8 us -> 67 us  [on_device(): pl.pallas_call(kernel, out_shape=(pltpu.VMEM((STEPS, TRIALS, SHARE), f32)...]
where the time goes in v4:
time: 69.3 us; the launch traced here: 68.9 us
  Pallas kernels  67 us (97%)
  local copies, waits for them, and re-layouts  1.28 us (2%)
    pallas_call x1, Pallas kernels, on_device(): pl.pallas_call(kernel, out_shape=(pltpu.VMEM((STEPS, TRIALS, SHARE), f32)...  67 us

profile of v4, /device:TPU:24, one launch (start us, length us, event | category | flops | bytes accessed | tf_op | source)
XLA Modules:
  0.0 68.9 jit_solution(5411344443147126562)
XLA Ops:
  0.6 67.0 %network_interval.1 = (f32[16,24,64]{2,1,0:T(8,128)S(1)}, f32[24,64]{1,0:T(8,128)S(1)}) custom-call(f32[64,1536]{1,0:T(8,128)} %hist_hbm.1, bf16[64,64,512]{2,1,0:T(8,128)(2,1)} %weights_hbm.1, s32[32,32]{1,0:T(8,128)} %delays_hbm.1, s32[32]{0:T(128)} %blocks_hbm.1, f32[24,64]{1,0:T(8,128)} %pot_hbm.1, f32[1,64]{1,0:T(1,128)} %bitcast.2, f32[1,64]{1,0:T(1,128)} %bitcast.3), custom_call_target="tpu_custom_call" | custom-call | tf_op jit(solution)/shard_map/network_interval/pallas_call | solution.py:388
  67.7 0.7 copy.11
  68.3 0.6 copy.12

commit v5 on v4

--- a/solution.py
+++ b/solution.py
@@ -60,18 +60,12 @@
     left = (block_at(y, z - 1, core), tgt)
 
     pairs = [
-        (hist_hbm, hist_ref), (blocks_hbm, blocks_ref), (delays_hbm, delays_ref), (weights_hbm, weights),
-        (pot_hbm, pot_ref), (leak_hbm, leak_ref), (drive_hbm, drive_ref),
+        (hist_hbm, hist_ref), (blocks_hbm, blocks_ref), (delays_hbm, delays_ref), (pot_hbm, pot_ref),
+        (leak_hbm, leak_ref), (drive_hbm, drive_ref), (weights_hbm, weights),
     ]
     loads = [pltpu.make_async_copy(a, b, in_sem.at[i]) for i, (a, b) in enumerate(pairs)]
-    for load in loads:
-        load.start()
-
+    loads[0].start()
     barrier = pltpu.get_barrier_semaphore()
-    for k in range(1, PEERS):
-        pl.semaphore_signal(barrier, 1, device_id=(peer_block(k, z), tgt), device_id_type=MESH)
-    for dx in range(1, RING):
-        pl.semaphore_signal(barrier, 1, device_id=x_peer(dx), device_id_type=MESH)
     pl.semaphore_signal(barrier, 1, device_id=across, device_id_type=MESH)
 
     @pl.when(z < CHAIN - 1)
@@ -81,6 +75,13 @@
     @pl.when(z > 0)
     def _():
         pl.semaphore_signal(barrier, 1, device_id=left, device_id_type=MESH)
+
+    for k in ORDER[:-1]:
+        pl.semaphore_signal(barrier, 1, device_id=(peer_block(k, z), tgt), device_id_type=MESH)
+    for dx in (2, 1, 3):
+        pl.semaphore_signal(barrier, 1, device_id=x_peer(dx), device_id_type=MESH)
+    for load in loads[1:-1]:
+        load.start()
 
     width = STEPS * TRIALS
     row = lax.broadcasted_iota(jnp.int32, (width, width), 0)
@@ -150,6 +151,7 @@
 
     for c in range(PASSES):
         pass_on(c, 0)
+    loads[-1].start()
     acc[...] = jnp.zeros_like(acc)
 
     sources = [block_at(y, zz, core) for zz in range(CHAIN)]
@@ -311,8 +313,7 @@
             rates_ref[s, mine, :] = jnp.maximum(membrane, 0.0) + jnp.log1p(jnp.exp(-jnp.abs(membrane)))
         last_ref[mine, :] = membrane
 
-    for load in loads[2:]:
-        load.wait()
+    loads[2].wait()
 
     def slot(k, _):
         def one(c, _):
@@ -327,6 +328,11 @@
         def two(c, _):
             t = k - OFFSET * c - LAG
 
+            @pl.when(jnp.logical_and(t == 0, c == 0))
+            def _():
+                for load in loads[3:]:
+                    load.wait()
+
             @pl.when(jnp.logical_and(t >= 0, t < CHAIN))
             def _():
                 product(c, t)
@@ -337,25 +343,11 @@
 
             return 0
 
-        def three(c, _):
-            t = k - OFFSET * c - LAG
-
-            @pl.when(t == CHAIN)
-            def _():
-                sum_x(c)
-
-            @pl.when(t == CHAIN + 1)
-            def _():
-                integrate(c)
-
-            return 0
-
         lax.fori_loop(0, PASSES, one, 0)
-        lax.fori_loop(0, PASSES, three, 0)
         lax.fori_loop(0, PASSES, two, 0)
         return 0
 
-    lax.fori_loop(0, OFFSET * (PASSES - 1) + CHAIN + LAG + 2, slot, 0)
+    lax.fori_loop(0, OFFSET * (PASSES - 1) + CHAIN + LAG, slot, 0)
 
     def drain(n, _):
         c, t = n // CHAIN, lax.rem(n, CHAIN)
@@ -370,15 +362,16 @@
             chain_copy(c, t, zs, False).wait_send()
 
         windows_copy(c, t).wait_send()
-
-        @pl.when(t == 0)
-        def _():
-            x_all(c).wait_send()
-            z_copy(c).wait_send()
-
         return 0
 
     lax.fori_loop(0, PASSES * CHAIN, drain, 0)
+    for c in range(PASSES):
+        sum_x(c)
+    for c in range(PASSES):
+        integrate(c)
+    for c in range(PASSES):
+        x_all(c).wait_send()
+        z_copy(c).wait_send()
 
 
 def on_device(history, weights, delays, area_blocks, potential, leak, drive):

time: 69.3 us -> 68.5 us (0.988)
  Pallas kernels: 67 us -> 65.6 us
    pallas_call x1, Pallas kernels: 67 us -> 65.6 us  [on_device(): pl.pallas_call(kernel, out_shape=(pltpu.VMEM((STEPS, TRIALS, SHARE), f32)...]
where the time goes in v5:
time: 68.5 us; the launch traced here: 67.5 us
  Pallas kernels  65.6 us (96%)
  local copies, waits for them, and re-layouts  1.28 us (2%)
    pallas_call x1, Pallas kernels, on_device(): pl.pallas_call(kernel, out_shape=(pltpu.VMEM((STEPS, TRIALS, SHARE), f32)...  65.6 us

profile of v5, /device:TPU:24, one launch (start us, length us, event | category | flops | bytes accessed | tf_op | source)
XLA Modules:
  0.0 67.5 jit_solution(11709636391773273050)
XLA Ops:
  0.6 65.6 %network_interval.1 = (f32[16,24,64]{2,1,0:T(8,128)S(1)}, f32[24,64]{1,0:T(8,128)S(1)}) custom-call(f32[64,1536]{1,0:T(8,128)} %hist_hbm.1, bf16[64,64,512]{2,1,0:T(8,128)(2,1)} %weights_hbm.1, s32[32,32]{1,0:T(8,128)} %delays_hbm.1, s32[32]{0:T(128)} %blocks_hbm.1, f32[24,64]{1,0:T(8,128)} %pot_hbm.1, f32[1,64]{1,0:T(1,128)} %bitcast.2, f32[1,64]{1,0:T(1,128)} %bitcast.3), custom_call_target="tpu_custom_call" | custom-call | tf_op jit(solution)/shard_map/network_interval/pallas_call | solution.py:381
  66.2 0.7 %copy.11 = f32[16,24,64]{2,1,0:T(8,128)} copy(f32[16,24,64]{2,1,0:T(8,128)S(1)} %get-tuple-element.2) | data formatting | bytes 196608
  66.9 0.6 copy.12

commit v6 on v5

--- a/solution.py
+++ b/solution.py
@@ -65,6 +65,7 @@
     ]
     loads = [pltpu.make_async_copy(a, b, in_sem.at[i]) for i, (a, b) in enumerate(pairs)]
     loads[0].start()
+    loads[1].start()
     barrier = pltpu.get_barrier_semaphore()
     pl.semaphore_signal(barrier, 1, device_id=across, device_id_type=MESH)
 
@@ -80,7 +81,7 @@
         pl.semaphore_signal(barrier, 1, device_id=(peer_block(k, z), tgt), device_id_type=MESH)
     for dx in (2, 1, 3):
         pl.semaphore_signal(barrier, 1, device_id=x_peer(dx), device_id_type=MESH)
-    for load in loads[1:-1]:
+    for load in loads[2:-1]:
         load.start()
 
     width = STEPS * TRIALS
@@ -89,6 +90,22 @@
     inner = lax.rem(col, LANES)
     wanted = (inner // GROUP) * TRIALS + (col // LANES) * GROUP + lax.rem(inner, GROUP)
     regroup = jnp.where(row == wanted, 1.0, 0.0).astype(jnp.bfloat16)
+    sources = [block_at(y, zz, core) for zz in range(CHAIN)]
+    targets = [peer_block(k, z) for k in range(PEERS)]
+
+    def count(a, carry):
+        edge, counts = carry[0] + blocks_ref[a], carry[1:]
+        more = [n + jnp.where(edge <= b, 1, 0) for n, b in zip(counts, sources + targets)]
+        return (edge, *more)
+
+    loads[1].wait()
+    counted = lax.fori_loop(0, AREAS, count, (jnp.int32(0),) * (1 + CHAIN + PEERS))[1:]
+    for i in range(CHAIN):
+        src_area[i] = jnp.minimum(counted[i], AREAS - 1)
+    for i in range(PEERS):
+        tgt_area[i] = jnp.minimum(counted[CHAIN + i], AREAS - 1)
+    acc[...] = jnp.zeros_like(acc)
+
     loads[0].wait()
     for q in range(SPANS):
         part = hist_ref[:, q * width : (q + 1) * width].astype(jnp.bfloat16)
@@ -152,22 +169,6 @@
     for c in range(PASSES):
         pass_on(c, 0)
     loads[-1].start()
-    acc[...] = jnp.zeros_like(acc)
-
-    sources = [block_at(y, zz, core) for zz in range(CHAIN)]
-    targets = [peer_block(k, z) for k in range(PEERS)]
-
-    def count(a, carry):
-        edge, counts = carry[0] + blocks_ref[a], carry[1:]
-        more = [n + jnp.where(edge <= b, 1, 0) for n, b in zip(counts, sources + targets)]
-        return (edge, *more)
-
-    loads[1].wait()
-    counted = lax.fori_loop(0, AREAS, count, (jnp.int32(0),) * (1 + CHAIN + PEERS))[1:]
-    for i in range(CHAIN):
-        src_area[i] = jnp.minimum(counted[i], AREAS - 1)
-    for i in range(PEERS):
-        tgt_area[i] = jnp.minimum(counted[CHAIN + i], AREAS - 1)
 
     lane = lax.broadcasted_iota(jnp.int32, (SHARE, LANES), 1)
 
@@ -364,9 +365,9 @@
         windows_copy(c, t).wait_send()
         return 0
 
-    lax.fori_loop(0, PASSES * CHAIN, drain, 0)
     for c in range(PASSES):
         sum_x(c)
+    lax.fori_loop(0, PASSES * CHAIN, drain, 0)
     for c in range(PASSES):
         integrate(c)
     for c in range(PASSES):

time: 68.5 us -> 67.6 us (0.987)
  Pallas kernels: 65.6 us -> 64.9 us
    pallas_call x1, Pallas kernels: 65.6 us -> 64.9 us  [on_device(): pl.pallas_call(kernel, out_shape=(pltpu.VMEM((STEPS, TRIALS, SHARE), f32)...]
where the time goes in v6:
time: 67.6 us; the launch traced here: 66.8 us
  Pallas kernels  64.9 us (96%)
  local copies, waits for them, and re-layouts  1.28 us (2%)
    pallas_call x1, Pallas kernels, on_device(): pl.pallas_call(kernel, out_shape=(pltpu.VMEM((STEPS, TRIALS, SHARE), f32)...  64.9 us

profile of v6, /device:TPU:24, one launch (start us, length us, event | category | flops | bytes accessed | tf_op | source)
XLA Modules:
  0.0 66.8 jit_solution(14858543285648439292)
XLA Ops:
  0.6 64.9 %network_interval.1 = (f32[16,24,64]{2,1,0:T(8,128)S(1)}, f32[24,64]{1,0:T(8,128)S(1)}) custom-call(f32[64,1536]{1,0:T(8,128)} %hist_hbm.1, bf16[64,64,512]{2,1,0:T(8,128)(2,1)} %weights_hbm.1, s32[32,32]{1,0:T(8,128)} %delays_hbm.1, s32[32]{0:T(128)} %blocks_hbm.1, f32[24,64]{1,0:T(8,128)} %pot_hbm.1, f32[1,64]{1,0:T(1,128)} %bitcast.2, f32[1,64]{1,0:T(1,128)} %bitcast.3), custom_call_target="tpu_custom_call" | custom-call | tf_op jit(solution)/shard_map/network_interval/pallas_call | solution.py:382
  65.5 0.7 %copy.11 = f32[16,24,64]{2,1,0:T(8,128)} copy(f32[16,24,64]{2,1,0:T(8,128)S(1)} %get-tuple-element.2) | data formatting | bytes 196608
  66.2 0.6 copy.12

commit v7 on v6

--- a/solution.py
+++ b/solution.py
@@ -86,7 +86,7 @@
 
     width = STEPS * TRIALS
     row = lax.broadcasted_iota(jnp.int32, (width, width), 0)
-    col = lax.broadcasted_iota(jnp.int32, (width, width), 1)
+    col = lax.broadcasted_iota(jnp.int32, (1, width), 1)
     inner = lax.rem(col, LANES)
     wanted = (inner // GROUP) * TRIALS + (col // LANES) * GROUP + lax.rem(inner, GROUP)
     regroup = jnp.where(row == wanted, 1.0, 0.0).astype(jnp.bfloat16)

time: 67.6 us -> 67.6 us (level)
  no operation moved by 1% of the time
where the time goes in v7:
time: 67.6 us; the launch traced here: 66.8 us
  Pallas kernels  64.9 us (96%)
  local copies, waits for them, and re-layouts  1.28 us (2%)
    pallas_call x1, Pallas kernels, on_device(): pl.pallas_call(kernel, out_shape=(pltpu.VMEM((STEPS, TRIALS, SHARE), f32)...  64.9 us

profile of v7, /device:TPU:24, one launch (start us, length us, event | category | flops | bytes accessed | tf_op | source)
XLA Modules:
  0.0 66.8 jit_solution(14858543285648439292)
XLA Ops:
  0.6 64.9 %network_interval.1 = (f32[16,24,64]{2,1,0:T(8,128)S(1)}, f32[24,64]{1,0:T(8,128)S(1)}) custom-call(f32[64,1536]{1,0:T(8,128)} %hist_hbm.1, bf16[64,64,512]{2,1,0:T(8,128)(2,1)} %weights_hbm.1, s32[32,32]{1,0:T(8,128)} %delays_hbm.1, s32[32]{0:T(128)} %blocks_hbm.1, f32[24,64]{1,0:T(8,128)} %pot_hbm.1, f32[1,64]{1,0:T(1,128)} %bitcast.2, f32[1,64]{1,0:T(1,128)} %bitcast.3), custom_call_target="tpu_custom_call" | custom-call | tf_op jit(solution)/shard_map/network_interval/pallas_call | solution.py:382
  65.5 0.7 %copy.11 = f32[16,24,64]{2,1,0:T(8,128)} copy(f32[16,24,64]{2,1,0:T(8,128)S(1)} %get-tuple-element.2) | data formatting | bytes 196608
  66.2 0.6 copy.12
